TPU v7x, 32 devices: a whole 2x2x4 slice. The times are simulated.
32 devices in a mesh: replica: 2 (over y), adapter: 4 (over z), tensor: 4 (over x, core).
Axes of the slice: x: 2, y: 2, z: 4, core: 2. Of those that a mesh axis runs over, the one named last changes fastest.
Arguments:
- tokens: bfloat16 [8192, 8192], P(('replica', 'adapter'), 'tensor'), parts along dimension 0, may hold values from -6 to 6
- value_base_matrix: bfloat16 [8192, 1024], P('tensor'), may hold values from -0.0625 to 0.0625
- adapter_down_table: bfloat16 [8, 8192, 64], P('adapter', 'tensor'), may hold values from -0.0625 to 0.0625
- adapter_up_table: bfloat16 [8, 64, 1024], P('adapter', None, 'tensor'), may hold values from -0.75 to 0.75
- adapter_per_block: int32 [128], P(('replica', 'adapter')), parts along dimension 0, may hold values from 0 to 7, as said below
- adapter_position: int32 [16], P('replica'), parts along dimension 0, may hold values from 0 to 7, as said below
Outputs:
- values_out: bfloat16 [8192, 1024], P(('replica', 'adapter'), 'tensor'), parts along dimension 0
There are 2 independent parts, one for each index of `replica`. A program takes and returns all parts, laid end to end along the dimension named above; an argument that names none is the same for every part. Nothing has to cross between parts.
Inputs may be any that keep to these rules, and one draw needn't show every extreme that they name: A permutation: adapter a lives in slot adapter_position[a]. The owner of a slot s is s // 2. `adapter_per_block`: of the 16 blocks of one device, at most 4 belong to adapters of one owner; in every draw some owner gets exactly 4 blocks from every device.
All inputs are finite; a program needn't handle non-finite values.
Results may differ from a plain program's by a relative error of at most 0.014.
Values may be sent and summed in bfloat16 or wider, within the bound.
A program may use at most 64 MiB of HBM per device.

v0:
```python
import jax
import jax.numpy as jnp
from jax import lax
from jax.sharding import PartitionSpec as P

BLK = 64


def shards(
    tokens,
    value_base_matrix,
    adapter_down_table,
    adapter_up_table,
    adapter_per_block,
    adapter_position,
):
    partial_value = jnp.dot(tokens, value_base_matrix, preferred_element_type=jnp.float32)
    base_projected = lax.psum_scatter(
        partial_value.astype(jnp.bfloat16), "tensor", scatter_dimension=1, tiled=True
    ).astype(jnp.float32)
    feat_width = tokens.shape[1]
    block_count = tokens.shape[0] // BLK
    all_adapters = adapter_position.shape[0]
    output_width = adapter_up_table.shape[2]
    token_groups_list = tokens.reshape(block_count, BLK, feat_width)
    matches = adapter_per_block[:, None] == jnp.arange(all_adapters, dtype=jnp.int32)[None, :]
    slot_per_block = jnp.sum(jnp.where(matches, adapter_position[None, :], 0), axis=1)
    table_down, table_up = (
        lax.all_gather(adapter_down_table, "adapter", axis=0, tiled=True),
        lax.all_gather(adapter_up_table, "adapter", axis=0, tiled=True),
    )
    down_rows = table_down[slot_per_block]
    up_rows = table_up[slot_per_block]
    shrunk_part = jnp.einsum(
        "bnd,bdr->bnr", token_groups_list, down_rows, preferred_element_type=jnp.float32
    )
    shrunk = lax.psum(shrunk_part.astype(jnp.bfloat16), "tensor")
    adapter_update = jnp.einsum(
        "bnr,bro->bno", shrunk, up_rows, preferred_element_type=jnp.float32
    ).astype(jnp.bfloat16)
    adapter_update = lax.optimization_barrier(adapter_update.reshape(tokens.shape[0], output_width))
    return (base_projected + adapter_update.astype(jnp.float32)).astype(jnp.bfloat16)


def solution(mesh):
    return jax.shard_map(
        shards,
        mesh=mesh,
        in_specs=(
            P(("replica", "adapter"), "tensor"),
            P("tensor", None),
            P("adapter", "tensor", None),
            P("adapter", None, "tensor"),
            P(("replica", "adapter")),
            P("replica"),
        ),
        out_specs=P(("replica", "adapter"), "tensor"),
        check_vma=False,
    )
```

profile of v0, /device:TPU:0, one launch (start us, length us, event | category | flops | bytes accessed | tf_op | source)
XLA Modules:
  0.0 140.8 jit_solution(1039426794394818799)
XLA Ops:
  6.5 0.0 all-gather.2.cloned.1.call-start
  6.5 0.7 all-gather.2.cloned.1.call-update
  7.3 0.0 all-reduce.2.cloned.1.call-start
  7.3 0.8 select_reduce_fusion
  8.1 49.5 %all-gather.2.cloned.1.call-done = bf16[8,2048,64]{1,2,0:T(8,128)(2,1)} async-done(((bf16[2,2048,64]{1,2,0:T(8,128)(2,1)}), bf16[8,2048,64]{1,2,0:T(8,128)(2,1)}) %all-gather.2.cloned.1.call-update) | async-done | bytes 2097168 | tf_op jit(solution)/shard_map/all_gather | solution.py:29
  57.6 4.3 %gather_fusion = bf16[16,2048,64]{1,2,0:T(8,128)(2,1)} fusion(bf16[8,2048,64]{1,2,0:T(8,128)(2,1)} %all-gather.2.cloned.1.call-done, s32[1024]{0:T(1024)S(1)} %pad_clamp_fusion), kind=kCustom, calls=%fused_computation | custom fusion | bytes 8388672 | tf_op jit(solution)/shard_map/gather | solution.py:32
  61.9 5.4 %fusion = bf16[16,64,64]{1,2,0:T(8,128)(2,1)} fusion(bf16[16,2048,64]{1,2,0:T(8,128)(2,1)} %gather_fusion, bf16[16,64,2048]{2,1,0:T(8,128)(2,1)} %bitcast.15), kind=kOutput, calls=%fused_computation.5 | convolution fusion | flops 268500992 | bytes 8519680 | tf_op jit(solution)/shard_map/bnd,bdr->bnr/dot_general | solution.py:34
  67.3 0.0 all-reduce.2.cloned.1.call-update
  67.4 0.0 copy-start
  67.4 0.0 reduce-scatter.2.cloned.1.call-start
  67.4 9.3 %convolution_convert_fusion = bf16[1024,1024]{1,0:T(8,128)(2,1)} fusion(bf16[1024,2048]{1,0:T(8,128)(2,1)} %param.6, bf16[2048,1024]{1,0:T(8,128)(2,1)} %param.7), kind=kOutput, calls=%fused_computation.2 | convolution fusion | flops 4296015872 | bytes 10485760 | tf_op jit(solution)/shard_map/dot_general | solution.py:17
  76.7 0.0 reduce-scatter.2.cloned.1.call-update
  76.8 0.0 copy-done
  76.8 14.2 %all_gather.7 = bf16[8,64,256]{2,1,0:T(8,128)(2,1)S(1)} all-gather(bf16[2,64,256]{2,1,0:T(8,128)(2,1)S(1)} %copy-done), channel_id=1, replica_groups=mesh['replica'=2,'adapter'=4,'tensor'=4] {'adapter'}, dimensions={0}, use_global_device_ids=true | all-gather | bytes 327680 | tf_op jit(solution)/shard_map/all_gather | solution.py:30
  90.9 0.6 gather_fusion.1
  91.5 6.7 %all-reduce.2.cloned.1.call-done = bf16[16,64,64]{1,2,0:T(8,128)(2,1)} async-done(((bf16[16,64,64]{1,2,0:T(8,128)(2,1)}), bf16[16,64,64]{1,2,0:T(8,128)(2,1)}) %all-reduce.2.cloned.1.call-update) | async-done | bytes 131088 | tf_op jit(solution)/shard_map/psum | solution.py:37
  98.2 1.3 convolution_convert_fusion.1
  99.5 32.8 %reduce-scatter.2.cloned.1.call-done = bf16[1024,256]{1,0:T(8,128)(2,1)} async-done(((bf16[1024,1024]{1,0:T(8,128)(2,1)}), bf16[1024,256]{1,0:T(8,128)(2,1)}) %reduce-scatter.2.cloned.1.call-update) | async-done | bytes 524304 | tf_op jit(solution)/shard_map/reduce_scatter | solution.py:18
  132.3 2.0 %add_convert_fusion = bf16[1024,256]{1,0:T(8,128)(2,1)} fusion(bf16[1024,256]{1,0:T(8,128)(2,1)S(1)} %bitcast.14, bf16[1024,256]{1,0:T(8,128)(2,1)} %reduce-scatter.2.cloned.1.call-done), kind=kLoop, calls=%fused_computation.6 | loop fusion | flops 1048576 | bytes 1572864 | tf_op jit(solution)/shard_map/convert_element_type | solution.py:42
  (2 shorter events, 0.0 us)
Async XLA Ops:
  6.5 51.1 %all-gather.2.cloned.1.call-start = ((), (), s32[]{:S(2)}) async-start(), calls=%async_computation.2 | async-start | bytes 2621440 | tf_op jit(solution)/shard_map/all_gather | solution.py:29
  7.3 91.0 %all-reduce.2.cloned.1.call-start = ((), (), s32[]{:S(2)}) async-start(), calls=%async_computation.3 | async-start | bytes 524288 | tf_op jit(solution)/shard_map/psum | solution.py:37
  67.4 9.4 %copy-start = (bf16[2,64,256]{2,1,0:T(8,128)(2,1)S(1)}, bf16[2,64,256]{2,1,0:T(8,128)(2,1)}, u32[]{:S(2)}) copy-start(bf16[2,64,256]{2,1,0:T(8,128)(2,1)} %param.9) | copy-start | bytes 196612
  67.4 65.0 %reduce-scatter.2.cloned.1.call-start = ((), (), s32[]{:S(2)}) async-start(), calls=%async_computation.1 | async-start | bytes 2621440 | tf_op jit(solution)/shard_map/reduce_scatter | solution.py:18
Sparse Core Ops, SparseCore 0:
  8.9 48.6 all-gather.1
  67.5 30.6 all-reduce.1
  100.9 31.3 reduce-scatter.1
where the time goes:
time: 141 us
  waiting for transfers between devices  89.8 us (64%)
  matrix products  16 us (11%)
  blocking collectives  14.2 us (10%)
  between operations  13.1 us (9%)
  local copies, waits for them, and re-layouts  4.92 us (3%)
  other arithmetic  2.73 us (2%)
    all_gather x1, waiting for transfers between devices, shards(): lax.all_gather(adapter_down_table, 'adapter', axis=0, tiled=True)  49.5 us
    reduce_scatter x1, waiting for transfers between devices, shards(): lax.psum_scatter(partial_value.astype(jnp.bfloat16), 'tensor', scatter_di...  32.8 us
    all_gather x1, blocking collectives, shards(): lax.all_gather(adapter_up_table, 'adapter', axis=0, tiled=True)  14.2 us
    dot_general x1, matrix products, shards(): jnp.dot(tokens, value_base_matrix, preferred_element_type=jnp.float32)  9.3 us
    psum x1, waiting for transfers between devices, shards(): shrunk = lax.psum(shrunk_part.astype(jnp.bfloat16), 'tensor')  6.67 us
    dot_general x1, matrix products, shards(): jnp.einsum('bnd,bdr->bnr', token_groups_list, down_rows, preferred_elemen...  5.41 us
    gather x1, local copies, waits for them, and re-layouts, shards(): down_rows = table_down[slot_per_block]  4.34 us
  transfers between devices with their start and end apart: 3, of which 3 were waited for; matrix products, arithmetic and copies ran while one was open for 8% of the time, Pallas kernels for 0%

commit v1 on v0

--- a/solution.py
+++ b/solution.py
@@ -1,9 +1,16 @@
+import functools
+
 import jax
 import jax.numpy as jnp
 from jax import lax
+from jax.experimental import pallas as pl
+from jax.experimental.pallas import tpu as pltpu
 from jax.sharding import PartitionSpec as P
 
 BLK = 64
+PIECES = 4
+ROWS = 256
+MESH = pl.DeviceIdType.MESH
 
 
 def shards(
@@ -42,9 +49,409 @@
     return (base_projected + adapter_update.astype(jnp.float32)).astype(jnp.bfloat16)
 
 
+def kernel(
+    owners,
+    apb,
+    apos,
+    tok_h,
+    base_h,
+    down_h,
+    up_h,
+    out,
+    tok,
+    base,
+    table,
+    toks,
+    sib_send,
+    sib_recv,
+    x_send,
+    x_recv,
+    total,
+    rank_f32,
+    rank_send,
+    rank_sib,
+    rank_x_send,
+    rank_x,
+    delta,
+    load_sem,
+    z_recv,
+    y_recv,
+    right_sem,
+    left_sem,
+    y_send,
+    base_sem,
+    rank_sem,
+):
+    y = lax.axis_index("replica")
+    z = lax.axis_index("adapter")
+    t = lax.axis_index("tensor")
+    core = lax.rem(t, 2)
+    sibling = t + 1 - 2 * core
+    far = lax.rem(t + 2, 4)
+    other_y = 1 - y
+    last = owners - 1
+
+    blocks, _, feats = tok.shape
+    quarter = out.shape[2]
+    per_owner = blocks // owners
+    owner_rows = per_owner * BLK
+    half_feats = feats // 2
+    width = 2 * BLK
+    piece = width // PIECES
+
+    loads = []
+    for h in range(2):
+        loads.append(pltpu.make_async_copy(
+            up_h.at[:, h * width:(h + 1) * width], table.at[z, h, :, :width], load_sem.at[2 * h]))
+        loads.append(pltpu.make_async_copy(
+            down_h.at[:, h * half_feats:(h + 1) * half_feats], table.at[z, h, :, width:], load_sem.at[2 * h + 1]))
+    loads.append(pltpu.make_async_copy(tok_h, tok, load_sem.at[4]))
+    loads.append(pltpu.make_async_copy(base_h, base, load_sem.at[5]))
+    for load in loads:
+        load.start()
+
+    barrier = pltpu.get_barrier_semaphore()
+
+    def greet(where):
+        pl.semaphore_signal(barrier, inc=1, device_id=where, device_id_type=MESH)
+
+    greet({"tensor": sibling})
+    greet({"tensor": far})
+    greet({"replica": other_y})
+
+    @pl.when(z > 0)
+    def _():
+        greet({"adapter": z - 1})
+
+    @pl.when(z < last)
+    def _():
+        greet({"adapter": z + 1})
+
+    for load in loads[:4]:
+        load.wait()
+    neighbours = jnp.minimum(z, 1) + jnp.minimum(last - z, 1)
+    pl.semaphore_wait(barrier, 3 + neighbours)
+
+    def part(owner, half, p):
+        return table.at[owner, half, p * piece:(p + 1) * piece, :]
+
+    def z_copy(owner, p, to, send):
+        ref = part(owner, y, p)
+        return pltpu.make_async_remote_copy(
+            src_ref=ref, dst_ref=ref, send_sem=send.at[owner, p], recv_sem=z_recv.at[owner, p],
+            device_id={"adapter": to}, device_id_type=MESH,
+        )
+
+    def y_copy(owner, p, half):
+        ref = part(owner, half, p)
+        return pltpu.make_async_remote_copy(
+            src_ref=ref, dst_ref=ref, send_sem=y_send.at[owner, p], recv_sem=y_recv.at[owner, p],
+            device_id={"replica": other_y}, device_id_type=MESH,
+        )
+
+    for p in range(PIECES):
+        @pl.when(z < last)
+        def _():
+            z_copy(z, p, z + 1, right_sem).start()
+
+        @pl.when(z > 0)
+        def _():
+            z_copy(z, p, z - 1, left_sem).start()
+
+    def forward(distance, p):
+        @pl.when(z >= distance)
+        def _():
+            owner = z - distance
+            z_copy(owner, p, z - 1, right_sem).wait_recv()
+
+            @pl.when(z < last)
+            def _():
+                z_copy(owner, p, z + 1, right_sem).start()
+            y_copy(owner, p, y).start()
+
+        @pl.when(z + distance <= last)
+        def _():
+            owner = z + distance
+            z_copy(owner, p, z + 1, left_sem).wait_recv()
+
+            @pl.when(z > 0)
+            def _():
+                z_copy(owner, p, z - 1, left_sem).start()
+            y_copy(owner, p, y).start()
+
+    def same(a, b):
+        return 1 - jnp.minimum((a - b) * (a - b), 1)
+
+    slot = [apos[apb[b]] for b in range(blocks)]
+    owner_of = [lax.div(s, 2) for s in slot]
+    place = []
+    for b in range(blocks):
+        before = jnp.int32(0)
+        for c in range(b):
+            before = before + same(owner_of[c], owner_of[b])
+        place.append(owner_of[b] * per_owner + before)
+
+    row_blocks = ROWS // BLK
+    row_steps = blocks // row_blocks
+
+    def base_piece(column, r):
+        at = pl.ds(r * row_blocks, row_blocks)
+        columns = pl.ds(pl.multiple_of(column * quarter, quarter), quarter)
+        rows = tok[at].reshape(ROWS, feats)
+        value = jnp.dot(rows, base[:, columns], preferred_element_type=jnp.float32)
+        return at, value.reshape(row_blocks, BLK, quarter)
+
+    def base_copy(src, dst, sem, to):
+        return pltpu.make_async_remote_copy(
+            src_ref=src, dst_ref=dst, send_sem=base_sem.at[2 * sem], recv_sem=base_sem.at[2 * sem + 1],
+            device_id={"tensor": to}, device_id_type=MESH,
+        )
+
+    sib_copy = [base_copy(sib_send.at[i], sib_recv.at[i], i, sibling) for i in range(2)]
+    x_copy = base_copy(x_send, x_recv, 2, far)
+
+    loads[4].wait()
+    loads[5].wait()
+
+    far_sibling = far + 1 - 2 * core
+
+    @pl.loop(0, row_steps)
+    def _(r):
+        at, value = base_piece(far_sibling, r)
+        sib_send[0, at] = value.astype(jnp.bfloat16)
+    sib_copy[0].start()
+    forward(1, 0)
+
+    @pl.loop(0, row_steps)
+    def _(r):
+        at, value = base_piece(far, r)
+        total[at] = value
+    sib_copy[0].wait_recv()
+    x_send[...] = (total[...] + sib_recv[0].astype(jnp.float32)).astype(jnp.bfloat16)
+    x_copy.start()
+    forward(1, 1)
+
+    @pl.loop(0, row_steps)
+    def _(r):
+        at, value = base_piece(sibling, r)
+        sib_send[1, at] = value.astype(jnp.bfloat16)
+    sib_copy[1].start()
+    forward(1, 2)
+
+    @pl.loop(0, row_steps)
+    def _(r):
+        at, value = base_piece(t, r)
+        total[at] = value
+    for p in range(3, PIECES):
+        forward(1, p)
+
+    parity = []
+    for s in range(blocks):
+        index, odd = jnp.int32(0), jnp.int32(0)
+        for b in range(blocks):
+            here = same(place[b], s)
+            index = index + here * b
+            odd = odd + here * lax.rem(slot[b], 2)
+        parity.append(odd)
+        toks[s] = tok[index]
+
+    lane_half = lax.div(lax.broadcasted_iota(jnp.int32, (BLK, width), 1), BLK)
+
+    def own_lanes(owner, k):
+        odd = jnp.int32(0)
+        for o in range(owners):
+            odd = odd + same(owner, o) * parity[o * per_owner + k]
+        return same(lane_half, odd).astype(jnp.float32)
+
+    def rank_copy(src, dst, owner, kind, to):
+        return pltpu.make_async_remote_copy(
+            src_ref=src.at[owner], dst_ref=dst.at[owner],
+            send_sem=rank_sem.at[2 * kind, owner], recv_sem=rank_sem.at[2 * kind + 1, owner],
+            device_id={"tensor": to}, device_id_type=MESH,
+        )
+
+    pairs = per_owner // 2
+
+    def shrink(owner):
+        rows = toks[pl.ds(owner * per_owner, per_owner)].reshape(owner_rows, feats)
+        value = jnp.zeros((owner_rows, width), jnp.float32)
+        for h in range(2):
+            value = value + lax.dot_general(
+                rows[:, h * half_feats:(h + 1) * half_feats], table[owner, h, :, width:],
+                (((1,), (1,)), ((), ())), preferred_element_type=jnp.float32,
+            )
+        picked = []
+        for k in range(per_owner):
+            rank = value[k * BLK:(k + 1) * BLK, :] * own_lanes(owner, k)
+            picked.append(rank[:, :BLK] + rank[:, BLK:])
+        packed = jnp.concatenate(
+            [jnp.concatenate(picked[:pairs], axis=0), jnp.concatenate(picked[pairs:], axis=0)], axis=1
+        )
+        rank_f32[owner] = packed
+        rank_send[owner] = packed.astype(jnp.bfloat16)
+        rank_copy(rank_send, rank_sib, owner, 0, sibling).start()
+
+    def chip_sum(owner):
+        rank_copy(rank_send, rank_sib, owner, 0, sibling).wait_recv()
+        value = rank_f32[owner] + rank_sib[owner].astype(jnp.float32)
+        rank_f32[owner] = value
+        rank_x_send[owner] = value.astype(jnp.bfloat16)
+        rank_copy(rank_x_send, rank_x, owner, 1, far).start()
+
+    def expand(owner):
+        rank_copy(rank_x_send, rank_x, owner, 1, far).wait_recv()
+        value = rank_f32[owner] + rank_x[owner].astype(jnp.float32)
+        spread = []
+        for k in range(per_owner):
+            column = (k // pairs) * BLK
+            rank = value[(k % pairs) * BLK:(k % pairs + 1) * BLK, column:column + BLK]
+            spread.append(jnp.concatenate([rank, rank], axis=1) * own_lanes(owner, k))
+        shrunk = jnp.concatenate(spread, axis=0).astype(jnp.bfloat16)
+        for h in range(2):
+            value = jnp.dot(shrunk, table[owner, h, :, :width], preferred_element_type=jnp.float32)
+            delta[pl.ds(owner * per_owner, per_owner), :, h * width:(h + 1) * width] = value.reshape(
+                per_owner, BLK, width
+            )
+
+    order = [z]
+    for j in range(1, owners):
+        pick = jnp.int32(0)
+        for me in range(owners):
+            by_distance = sorted((o for o in range(owners) if o != me), key=lambda o: abs(o - me))
+            pick = jnp.where(z == me, by_distance[j - 1], pick)
+        order.append(pick)
+
+    def y_wait(owner):
+        for p in range(PIECES):
+            y_copy(owner, p, other_y).wait_recv()
+
+    shrink(order[0])
+    for p in range(PIECES):
+        forward(2, p)
+        if p == 0:
+            chip_sum(order[0])
+        if p == 1:
+            expand(order[0])
+    y_wait(order[1])
+    shrink(order[1])
+    forward(3, 0)
+    chip_sum(order[1])
+    y_wait(order[2])
+    shrink(order[2])
+    forward(3, 1)
+    expand(order[1])
+    chip_sum(order[2])
+    forward(3, 2)
+    sib_copy[1].wait_recv()
+    x_copy.wait_recv()
+    total[...] = total[...] + sib_recv[1].astype(jnp.float32) + x_recv[...].astype(jnp.float32)
+    for p in range(3, PIECES):
+        forward(3, p)
+    expand(order[2])
+    y_wait(order[3])
+    shrink(order[3])
+    chip_sum(order[3])
+    expand(order[3])
+    for b in range(blocks):
+        out[b] = (total[b] + delta[place[b]]).astype(jnp.bfloat16)
+
+    for copy in (*sib_copy, x_copy):
+        copy.wait_send()
+    for owner in range(owners):
+        rank_copy(rank_send, rank_sib, owner, 0, sibling).wait_send()
+        rank_copy(rank_x_send, rank_x, owner, 1, far).wait_send()
+        for p in range(PIECES):
+            @pl.when(owner != z)
+            def _():
+                y_copy(owner, p, y).wait_send()
+
+            @pl.when(jnp.logical_and(owner <= z, z < last))
+            def _():
+                z_copy(owner, p, z + 1, right_sem).wait_send()
+
+            @pl.when(jnp.logical_and(owner >= z, z > 0))
+            def _():
+                z_copy(owner, p, z - 1, left_sem).wait_send()
+
+
+def fused(owners, tokens, value_base_matrix, down_table, up_table, adapter_per_block, adapter_position):
+    rows, feats = tokens.shape
+    quarter = up_table.shape[2]
+    out_columns = value_base_matrix.shape[1]
+    width = 2 * BLK
+    blocks = rows // BLK
+    owner_rows = rows // owners
+    tokens = tokens.reshape(blocks, BLK, feats)
+    down_rows = down_table.transpose(0, 2, 1).reshape(width, feats)
+    up_rows = up_table.reshape(width, quarter)
+    by_block = (blocks, BLK, quarter)
+    any_spec = pl.BlockSpec(memory_space=pl.ANY)
+    smem = pl.BlockSpec(memory_space=pltpu.SMEM)
+    rank_shape = (owners, owner_rows // 2, width)
+    dma = pltpu.SemaphoreType.DMA
+    out = pl.pallas_call(
+        functools.partial(kernel, owners),
+        out_shape=jax.ShapeDtypeStruct(by_block, jnp.bfloat16),
+        in_specs=[smem, smem, any_spec, any_spec, any_spec, any_spec],
+        out_specs=pl.BlockSpec(memory_space=pltpu.VMEM),
+        scratch_shapes=[
+            pltpu.VMEM((blocks, BLK, feats), jnp.bfloat16),
+            pltpu.VMEM((feats, out_columns), jnp.bfloat16),
+            pltpu.VMEM((owners, 2, width, width + feats // 2), jnp.bfloat16),
+            pltpu.VMEM((blocks, BLK, feats), jnp.bfloat16),
+            pltpu.VMEM((2, *by_block), jnp.bfloat16),
+            pltpu.VMEM((2, *by_block), jnp.bfloat16),
+            pltpu.VMEM(by_block, jnp.bfloat16),
+            pltpu.VMEM(by_block, jnp.bfloat16),
+            pltpu.VMEM(by_block, jnp.float32),
+            pltpu.VMEM(rank_shape, jnp.float32),
+            pltpu.VMEM(rank_shape, jnp.bfloat16),
+            pltpu.VMEM(rank_shape, jnp.bfloat16),
+            pltpu.VMEM(rank_shape, jnp.bfloat16),
+            pltpu.VMEM(rank_shape, jnp.bfloat16),
+            pltpu.VMEM(by_block, jnp.float32),
+            dma((6,)),
+            dma((owners, PIECES)),
+            dma((owners, PIECES)),
+            dma((owners, PIECES)),
+            dma((owners, PIECES)),
+            dma((owners, PIECES)),
+            dma((6,)),
+            dma((4, owners)),
+        ],
+        compiler_params=pltpu.CompilerParams(
+            collective_id=0, has_side_effects=True, vmem_limit_bytes=48 * 1024 * 1024
+        ),
+        cost_estimate=pl.CostEstimate(
+            flops=2 * rows * feats * (out_columns + width),
+            bytes_accessed=2 * (rows * feats + feats * out_columns + rows * quarter),
+            transcendentals=0,
+        ),
+    )(adapter_per_block, adapter_position, tokens, value_base_matrix, down_rows, up_rows)
+    return out.reshape(rows, quarter)
+
+
 def solution(mesh):
+    axes = mesh.shape
+
+    def run(tokens, value_base_matrix, down_table, up_table, adapter_per_block, adapter_position):
+        fits = (
+            axes["tensor"] == 4
+            and axes["replica"] == 2
+            and axes["adapter"] == 4
+            and down_table.shape[0] == 2
+            and tokens.shape[0] == 16 * BLK
+            and up_table.shape[1:] == (BLK, 4 * BLK)
+            and tokens.shape[1] % 512 == 0
+        )
+        if fits:
+            return fused(
+                axes["adapter"], tokens, value_base_matrix, down_table, up_table, adapter_per_block, adapter_position
+            )
+        return shards(tokens, value_base_matrix, down_table, up_table, adapter_per_block, adapter_position)
+
     return jax.shard_map(
-        shards,
+        run,
         mesh=mesh,
         in_specs=(
             P(("replica", "adapter"), "tensor"),

time: 141 us -> 46.3 us (0.33)
  waiting for transfers between devices: 89.8 us -> 0 us
  Pallas kernels: 0 us -> 39.9 us
  matrix products: 16 us -> 0 us
  blocking collectives: 14.2 us -> 0 us
  between operations: 13.1 us -> 0.01 us
  other arithmetic: 2.73 us -> 0 us
    all_gather x1 -> x0, waiting for transfers between devices: 49.5 us -> none  [shards(): lax.all_gather(adapter_down_table, 'adapter', axis=0, tiled=True)]
    pallas_call x0 -> x1, Pallas kernels: none -> 39.9 us  [fused(): pl.pallas_call(functools.partial(kernel, owners), out_shape=jax.ShapeDtyp...]
    reduce_scatter x1 -> x0, waiting for transfers between devices: 32.8 us -> none  [shards(): lax.psum_scatter(partial_value.astype(jnp.bfloat16), 'tensor', scatter_di...]
    dot_general x3 -> x0, matrix products: 16 us -> none  [the longest x1 9.3 us: shards(): jnp.dot(tokens, value_base_matrix, preferred_element_type=jnp.float32)]
    all_gather x1 -> x0, blocking collectives: 14.2 us -> none  [shards(): lax.all_gather(adapter_up_table, 'adapter', axis=0, tiled=True)]
    psum x1 -> x0, waiting for transfers between devices: 6.67 us -> none  [shards(): shrunk = lax.psum(shrunk_part.astype(jnp.bfloat16), 'tensor')]
    unnamed x2 -> x11, local copies, waits for them, and re-layouts: 0.01 us -> 6.17 us
    gather x2 -> x0, local copies, waits for them, and re-layouts: 4.92 us -> none  [the longest x1 4.34 us: shards(): down_rows = table_down[slot_per_block]]
  transfers between devices with their start and end apart: 3 -> 0, of which waited for: 3 -> 0; matrix products, arithmetic and copies ran while one was open for 8% -> 0% of each run, Pallas kernels for 0% -> 0%
where the time goes in v1:
time: 46.3 us; the launch traced here: 46.1 us
  Pallas kernels  39.9 us (86%)
  local copies, waits for them, and re-layouts  6.17 us (13%)
    pallas_call x1, Pallas kernels, fused(): pl.pallas_call(functools.partial(kernel, owners), out_shape=jax.ShapeDtyp...  39.9 us
    unnamed x11, local copies, waits for them, and re-layouts  6.17 us

profile of v1, /device:TPU:0, one launch (start us, length us, event | category | flops | bytes accessed | tf_op | source)
XLA Modules:
  0.0 46.1 jit_solution(3850705535300729951)
XLA Ops:
  0.0 0.0 copy-start
  0.0 2.2 %copy-done = bf16[1024,2048]{1,0:T(8,128)(2,1)S(1)} copy-done((bf16[1024,2048]{1,0:T(8,128)(2,1)S(1)}, bf16[1024,2048]{1,0:T(8,128)(2,1)}, u32[]{:S(2)}) %copy-start) | copy-done | bytes 4194328
  2.2 0.0 copy-start.1
  2.2 1.0 %copy-done.1 = bf16[2,2048,64]{1,2,0:T(8,128)(2,1)S(1)} copy-done((bf16[2,2048,64]{1,2,0:T(8,128)(2,1)S(1)}, bf16[2,2048,64]{1,2,0:T(8,128)(2,1)}, u32[]{:S(2)}) %copy-start.1) | copy-done | bytes 524312
  3.2 0.0 copy-start.2
  3.2 0.8 %copy-done.2 = bf16[2,64,256]{2,1,0:T(8,128)(2,1)S(1)} copy-done((bf16[2,64,256]{2,1,0:T(8,128)(2,1)S(1)}, bf16[2,64,256]{2,1,0:T(8,128)(2,1)}, u32[]{:S(2)}) %copy-start.2) | copy-done | bytes 65560
  4.1 0.0 copy-start.3
  4.1 0.7 %copy-done.3 = s32[16]{0:T(128)S(1)} copy-done((s32[16]{0:T(128)S(1)}, s32[16]{0:T(128)}, u32[]{:S(2)}) %copy-start.3) | copy-done | bytes 88
  4.7 0.0 copy-start.4
  4.7 0.7 %copy-done.4 = s32[8]{0:T(128)S(1)} copy-done((s32[8]{0:T(128)S(1)}, s32[8]{0:T(128)}, u32[]{:S(2)}) %copy-start.4) | copy-done | bytes 56
  5.4 39.9 %shard_map.64 = bf16[16,64,256]{2,1,0:T(8,128)(2,1)S(1)} custom-call(s32[16]{0:T(128)S(1)} %copy-done.3, s32[8]{0:T(128)S(1)} %copy-done.4, bf16[16,64,2048]{2,1,0:T(8,128)(2,1)S(1)} %bitcast.7, bf16[2048,1024]{1,0:T(8,128)(2,1)} %base_h.1, bf16[128,2048]{1,0:T(8,128)(2,1)S(1)} %bitcast.8, bf16[128,256]{1,0:T(8,128)(2,1)S(1)} %bitcast.9), custom_call_target="tpu_custom_call" | custom-call | flops 4831838208 | bytes 8912896 | tf_op jit(solution)/shard_map/pallas_call | solution.py:392
  45.3 0.8 %copy.8 = bf16[1024,256]{1,0:T(8,128)(2,1)} copy(bf16[1024,256]{1,0:T(8,128)(2,1)S(1)} %bitcast.6) | data formatting | bytes 1048576
Async XLA Ops:
  0.0 2.2 %copy-start = (bf16[1024,2048]{1,0:T(8,128)(2,1)S(1)}, bf16[1024,2048]{1,0:T(8,128)(2,1)}, u32[]{:S(2)}) copy-start(bf16[1024,2048]{1,0:T(8,128)(2,1)} %param.6) | copy-start | bytes 12582916
  2.2 1.0 %copy-start.1 = (bf16[2,2048,64]{1,2,0:T(8,128)(2,1)S(1)}, bf16[2,2048,64]{1,2,0:T(8,128)(2,1)}, u32[]{:S(2)}) copy-start(bf16[2,2048,64]{1,2,0:T(8,128)(2,1)} %param.8) | copy-start | bytes 1572868
  3.2 0.8 %copy-start.2 = (bf16[2,64,256]{2,1,0:T(8,128)(2,1)S(1)}, bf16[2,64,256]{2,1,0:T(8,128)(2,1)}, u32[]{:S(2)}) copy-start(bf16[2,64,256]{2,1,0:T(8,128)(2,1)} %param.9) | copy-start | bytes 196612
  4.1 0.7 %copy-start.3 = (s32[16]{0:T(128)S(1)}, s32[16]{0:T(128)}, u32[]{:S(2)}) copy-start(s32[16]{0:T(128)} %apb.1) | copy-start | bytes 196
  4.7 0.7 %copy-start.4 = (s32[8]{0:T(128)S(1)}, s32[8]{0:T(128)}, u32[]{:S(2)}) copy-start(s32[8]{0:T(128)} %apos.1) | copy-start | bytes 100

commit v2 on v1

--- a/solution.py
+++ b/solution.py
@@ -9,7 +9,7 @@
 
 BLK = 64
 PIECES = 4
-ROWS = 256
+ROWS = 512
 MESH = pl.DeviceIdType.MESH
 
 
@@ -51,8 +51,8 @@
 
 def kernel(
     owners,
-    apb,
-    apos,
+    apb_h,
+    apos_h,
     tok_h,
     base_h,
     down_h,
@@ -72,7 +72,10 @@
     rank_sib,
     rank_x_send,
     rank_x,
+    last_recv,
     delta,
+    apb,
+    apos,
     load_sem,
     z_recv,
     y_recv,
@@ -81,6 +84,7 @@
     y_send,
     base_sem,
     rank_sem,
+    last_sem,
 ):
     y = lax.axis_index("replica")
     z = lax.axis_index("adapter")
@@ -88,6 +92,7 @@
     core = lax.rem(t, 2)
     sibling = t + 1 - 2 * core
     far = lax.rem(t + 2, 4)
+    far_sibling = far + 1 - 2 * core
     other_y = 1 - y
     last = owners - 1
 
@@ -107,6 +112,8 @@
             down_h.at[:, h * half_feats:(h + 1) * half_feats], table.at[z, h, :, width:], load_sem.at[2 * h + 1]))
     loads.append(pltpu.make_async_copy(tok_h, tok, load_sem.at[4]))
     loads.append(pltpu.make_async_copy(base_h, base, load_sem.at[5]))
+    loads.append(pltpu.make_async_copy(apb_h, apb, load_sem.at[6]))
+    loads.append(pltpu.make_async_copy(apos_h, apos, load_sem.at[7]))
     for load in loads:
         load.start()
 
@@ -117,6 +124,7 @@
 
     greet({"tensor": sibling})
     greet({"tensor": far})
+    greet({"tensor": far_sibling})
     greet({"replica": other_y})
 
     @pl.when(z > 0)
@@ -130,7 +138,7 @@
     for load in loads[:4]:
         load.wait()
     neighbours = jnp.minimum(z, 1) + jnp.minimum(last - z, 1)
-    pl.semaphore_wait(barrier, 3 + neighbours)
+    pl.semaphore_wait(barrier, 4 + neighbours)
 
     def part(owner, half, p):
         return table.at[owner, half, p * piece:(p + 1) * piece, :]
@@ -182,6 +190,8 @@
     def same(a, b):
         return 1 - jnp.minimum((a - b) * (a - b), 1)
 
+    loads[6].wait()
+    loads[7].wait()
     slot = [apos[apb[b]] for b in range(blocks)]
     owner_of = [lax.div(s, 2) for s in slot]
     place = []
@@ -207,43 +217,36 @@
             device_id={"tensor": to}, device_id_type=MESH,
         )
 
-    sib_copy = [base_copy(sib_send.at[i], sib_recv.at[i], i, sibling) for i in range(2)]
-    x_copy = base_copy(x_send, x_recv, 2, far)
+    halves = [pl.ds(i * row_blocks, row_blocks) for i in range(row_steps)]
+    far_sib_copy = [
+        base_copy(sib_send.at[0, half], sib_recv.at[0, half], i, sibling) for i, half in enumerate(halves)
+    ]
+    x_copy = [base_copy(x_send.at[half], x_recv.at[half], row_steps + i, far) for i, half in enumerate(halves)]
+    sib_copy = base_copy(sib_send.at[1], sib_recv.at[1], 2 * row_steps, sibling)
 
     loads[4].wait()
     loads[5].wait()
 
-    far_sibling = far + 1 - 2 * core
-
-    @pl.loop(0, row_steps)
-    def _(r):
-        at, value = base_piece(far_sibling, r)
+    for i in range(row_steps):
+        at, value = base_piece(far_sibling, i)
         sib_send[0, at] = value.astype(jnp.bfloat16)
-    sib_copy[0].start()
+        far_sib_copy[i].start()
     forward(1, 0)
-
-    @pl.loop(0, row_steps)
-    def _(r):
-        at, value = base_piece(far, r)
-        total[at] = value
-    sib_copy[0].wait_recv()
-    x_send[...] = (total[...] + sib_recv[0].astype(jnp.float32)).astype(jnp.bfloat16)
-    x_copy.start()
-    forward(1, 1)
-
-    @pl.loop(0, row_steps)
-    def _(r):
-        at, value = base_piece(sibling, r)
+    for i in range(row_steps):
+        at, value = base_piece(far, i)
+        far_sib_copy[i].wait_recv()
+        x_send[at] = (value + sib_recv[0, at].astype(jnp.float32)).astype(jnp.bfloat16)
+        x_copy[i].start()
+        forward(1, 1 + i)
+
+    at, value = base_piece(sibling, 0)
+    sib_send[1, at] = value.astype(jnp.bfloat16)
+    for p in range(1 + row_steps, PIECES):
+        forward(1, p)
+    for i in range(1, row_steps):
+        at, value = base_piece(sibling, i)
         sib_send[1, at] = value.astype(jnp.bfloat16)
-    sib_copy[1].start()
-    forward(1, 2)
-
-    @pl.loop(0, row_steps)
-    def _(r):
-        at, value = base_piece(t, r)
-        total[at] = value
-    for p in range(3, PIECES):
-        forward(1, p)
+    sib_copy.start()
 
     parity = []
     for s in range(blocks):
@@ -272,7 +275,17 @@
 
     pairs = per_owner // 2
 
-    def shrink(owner):
+    def last_copies(owner):
+        return [
+            pltpu.make_async_remote_copy(
+                src_ref=rank_send.at[owner], dst_ref=last_recv.at[i],
+                send_sem=last_sem.at[2 * i], recv_sem=last_sem.at[2 * i + 1],
+                device_id={"tensor": to}, device_id_type=MESH,
+            )
+            for i, to in enumerate((far_sibling, far, sibling))
+        ]
+
+    def shrink(owner, in_one_step=False):
         rows = toks[pl.ds(owner * per_owner, per_owner)].reshape(owner_rows, feats)
         value = jnp.zeros((owner_rows, width), jnp.float32)
         for h in range(2):
@@ -289,7 +302,11 @@
         )
         rank_f32[owner] = packed
         rank_send[owner] = packed.astype(jnp.bfloat16)
-        rank_copy(rank_send, rank_sib, owner, 0, sibling).start()
+        if in_one_step:
+            for copy in last_copies(owner):
+                copy.start()
+        else:
+            rank_copy(rank_send, rank_sib, owner, 0, sibling).start()
 
     def chip_sum(owner):
         rank_copy(rank_send, rank_sib, owner, 0, sibling).wait_recv()
@@ -298,9 +315,16 @@
         rank_x_send[owner] = value.astype(jnp.bfloat16)
         rank_copy(rank_x_send, rank_x, owner, 1, far).start()
 
-    def expand(owner):
-        rank_copy(rank_x_send, rank_x, owner, 1, far).wait_recv()
-        value = rank_f32[owner] + rank_x[owner].astype(jnp.float32)
+    def expand(owner, in_one_step=False):
+        if in_one_step:
+            for copy in last_copies(owner):
+                copy.wait_recv()
+            value = rank_f32[owner]
+            for i in range(3):
+                value = value + last_recv[i].astype(jnp.float32)
+        else:
+            rank_copy(rank_x_send, rank_x, owner, 1, far).wait_recv()
+            value = rank_f32[owner] + rank_x[owner].astype(jnp.float32)
         spread = []
         for k in range(per_owner):
             column = (k // pairs) * BLK
@@ -325,41 +349,47 @@
         for p in range(PIECES):
             y_copy(owner, p, other_y).wait_recv()
 
+    forward(2, 0)
     shrink(order[0])
-    for p in range(PIECES):
+    forward(2, 1)
+    for i in range(row_steps):
+        at, value = base_piece(t, i)
+        total[at] = value
+        forward(2, 2 + i)
+    for p in range(2 + row_steps, PIECES):
         forward(2, p)
-        if p == 0:
-            chip_sum(order[0])
-        if p == 1:
-            expand(order[0])
+    chip_sum(order[0])
     y_wait(order[1])
     shrink(order[1])
+    sib_copy.wait_recv()
+    total[...] = total[...] + sib_recv[1].astype(jnp.float32)
     forward(3, 0)
+    expand(order[0])
     chip_sum(order[1])
+    forward(3, 1)
     y_wait(order[2])
     shrink(order[2])
-    forward(3, 1)
+    forward(3, 2)
     expand(order[1])
-    chip_sum(order[2])
-    forward(3, 2)
-    sib_copy[1].wait_recv()
-    x_copy.wait_recv()
-    total[...] = total[...] + sib_recv[1].astype(jnp.float32) + x_recv[...].astype(jnp.float32)
     for p in range(3, PIECES):
         forward(3, p)
+    chip_sum(order[2])
+    for i, half in enumerate(halves):
+        x_copy[i].wait_recv()
+        total[half] = total[half] + x_recv[half].astype(jnp.float32)
+    y_wait(order[3])
+    shrink(order[3], in_one_step=True)
     expand(order[2])
-    y_wait(order[3])
-    shrink(order[3])
-    chip_sum(order[3])
-    expand(order[3])
+    expand(order[3], in_one_step=True)
     for b in range(blocks):
         out[b] = (total[b] + delta[place[b]]).astype(jnp.bfloat16)
 
-    for copy in (*sib_copy, x_copy):
+    for copy in (*far_sib_copy, *x_copy, sib_copy, *last_copies(order[3])):
         copy.wait_send()
-    for owner in range(owners):
+    for owner in order[:3]:
         rank_copy(rank_send, rank_sib, owner, 0, sibling).wait_send()
         rank_copy(rank_x_send, rank_x, owner, 1, far).wait_send()
+    for owner in range(owners):
         for p in range(PIECES):
             @pl.when(owner != z)
             def _():
@@ -385,14 +415,13 @@
     down_rows = down_table.transpose(0, 2, 1).reshape(width, feats)
     up_rows = up_table.reshape(width, quarter)
     by_block = (blocks, BLK, quarter)
-    any_spec = pl.BlockSpec(memory_space=pl.ANY)
-    smem = pl.BlockSpec(memory_space=pltpu.SMEM)
+    hbm = pl.BlockSpec(memory_space=pltpu.HBM)
     rank_shape = (owners, owner_rows // 2, width)
     dma = pltpu.SemaphoreType.DMA
     out = pl.pallas_call(
         functools.partial(kernel, owners),
         out_shape=jax.ShapeDtypeStruct(by_block, jnp.bfloat16),
-        in_specs=[smem, smem, any_spec, any_spec, any_spec, any_spec],
+        in_specs=[hbm] * 6,
         out_specs=pl.BlockSpec(memory_space=pltpu.VMEM),
         scratch_shapes=[
             pltpu.VMEM((blocks, BLK, feats), jnp.bfloat16),
@@ -409,18 +438,22 @@
             pltpu.VMEM(rank_shape, jnp.bfloat16),
             pltpu.VMEM(rank_shape, jnp.bfloat16),
             pltpu.VMEM(rank_shape, jnp.bfloat16),
+            pltpu.VMEM((3, *rank_shape[1:]), jnp.bfloat16),
             pltpu.VMEM(by_block, jnp.float32),
-            dma((6,)),
+            pltpu.SMEM(adapter_per_block.shape, jnp.int32),
+            pltpu.SMEM(adapter_position.shape, jnp.int32),
+            dma((8,)),
             dma((owners, PIECES)),
             dma((owners, PIECES)),
             dma((owners, PIECES)),
             dma((owners, PIECES)),
             dma((owners, PIECES)),
+            dma((2 * (2 * rows // ROWS + 1),)),
+            dma((4, owners)),
             dma((6,)),
-            dma((4, owners)),
         ],
         compiler_params=pltpu.CompilerParams(
-            collective_id=0, has_side_effects=True, vmem_limit_bytes=48 * 1024 * 1024
+            collective_id=0, has_side_effects=True, vmem_limit_bytes=64 * 1024 * 1024
         ),
         cost_estimate=pl.CostEstimate(
             flops=2 * rows * feats * (out_columns + width),

time: 46.3 us -> 38.6 us (0.83)
  local copies, waits for them, and re-layouts: 6.17 us -> 1.87 us
  Pallas kernels: 39.9 us -> 36.6 us
    unnamed x11 -> x1, local copies, waits for them, and re-layouts: 6.17 us -> 1.87 us
    pallas_call x1, Pallas kernels: 39.9 us -> 36.6 us  [fused(): pl.pallas_call(functools.partial(kernel, owners), out_shape=jax.ShapeDtyp...]
where the time goes in v2:
time: 38.6 us; the launch traced here: 38.5 us
  Pallas kernels  36.6 us (95%)
  local copies, waits for them, and re-layouts  1.87 us (5%)
    pallas_call x1, Pallas kernels, fused(): pl.pallas_call(functools.partial(kernel, owners), out_shape=jax.ShapeDtyp...  36.6 us
    unnamed x1, local copies, waits for them, and re-layouts  1.87 us

profile of v2, /device:TPU:0, one launch (start us, length us, event | category | flops | bytes accessed | tf_op | source)
XLA Modules:
  0.0 38.5 jit_solution(8393594389993272834)
XLA Ops:
  0.0 36.6 %shard_map.64 = bf16[16,64,256]{2,1,0:T(8,128)(2,1)} custom-call(s32[16]{0:T(128)} %apb_h.1, s32[8]{0:T(128)} %apos_h.1, bf16[16,64,2048]{2,1,0:T(8,128)(2,1)} %bitcast.7, bf16[2048,1024]{1,0:T(8,128)(2,1)} %base_h.1, bf16[128,2048]{1,0:T(8,128)(2,1)} %bitcast.8, bf16[128,256]{1,0:T(8,128)(2,1)} %bitcast.9), custom_call_target="tpu_custom_call" | custom-call | flops 4831838208 | bytes 8912896 | tf_op jit(solution)/shard_map/pallas_call | solution.py:421
  36.6 1.9 %copy.8 = bf16[1024,256]{1,0:T(8,128)(2,1)} copy(bf16[1024,256]{1,0:T(8,128)(2,1)} %bitcast.6) | data formatting | bytes 1048576

commit v3 on v2

--- a/solution.py
+++ b/solution.py
@@ -114,7 +114,7 @@
     loads.append(pltpu.make_async_copy(base_h, base, load_sem.at[5]))
     loads.append(pltpu.make_async_copy(apb_h, apb, load_sem.at[6]))
     loads.append(pltpu.make_async_copy(apos_h, apos, load_sem.at[7]))
-    for load in loads:
+    for load in (*loads[:4], *loads[6:]):
         load.start()
 
     barrier = pltpu.get_barrier_semaphore()
@@ -137,6 +137,8 @@
 
     for load in loads[:4]:
         load.wait()
+    for load in loads[4:6]:
+        load.start()
     neighbours = jnp.minimum(z, 1) + jnp.minimum(last - z, 1)
     pl.semaphore_wait(barrier, 4 + neighbours)
 
@@ -144,11 +146,15 @@
         return table.at[owner, half, p * piece:(p + 1) * piece, :]
 
     def z_copy(owner, p, to, send):
-        ref = part(owner, y, p)
+        ref = part(owner, y, p) if p < PIECES else part(owner, other_y, PIECES - 1)
         return pltpu.make_async_remote_copy(
             src_ref=ref, dst_ref=ref, send_sem=send.at[owner, p], recv_sem=z_recv.at[owner, p],
             device_id={"adapter": to}, device_id_type=MESH,
         )
+
+    def by_y(owner, p):
+        outer = jnp.logical_or(owner == 0, owner == last)
+        return True if p < PIECES - 1 else jnp.logical_not(outer)
 
     def y_copy(owner, p, half):
         ref = part(owner, half, p)
@@ -157,17 +163,17 @@
             device_id={"replica": other_y}, device_id_type=MESH,
         )
 
-    for p in range(PIECES):
-        @pl.when(z < last)
+    for p in range(PIECES + 1):
+        @pl.when(z == 0 if p == PIECES else z < last)
         def _():
             z_copy(z, p, z + 1, right_sem).start()
 
-        @pl.when(z > 0)
+        @pl.when(z == last if p == PIECES else z > 0)
         def _():
             z_copy(z, p, z - 1, left_sem).start()
 
     def forward(distance, p):
-        @pl.when(z >= distance)
+        @pl.when(z == distance if p == PIECES else z >= distance)
         def _():
             owner = z - distance
             z_copy(owner, p, z - 1, right_sem).wait_recv()
@@ -175,9 +181,12 @@
             @pl.when(z < last)
             def _():
                 z_copy(owner, p, z + 1, right_sem).start()
-            y_copy(owner, p, y).start()
-
-        @pl.when(z + distance <= last)
+            if p < PIECES:
+                @pl.when(by_y(owner, p))
+                def _():
+                    y_copy(owner, p, y).start()
+
+        @pl.when(z + distance == last if p == PIECES else z + distance <= last)
         def _():
             owner = z + distance
             z_copy(owner, p, z + 1, left_sem).wait_recv()
@@ -185,7 +194,10 @@
             @pl.when(z > 0)
             def _():
                 z_copy(owner, p, z - 1, left_sem).start()
-            y_copy(owner, p, y).start()
+            if p < PIECES:
+                @pl.when(by_y(owner, p))
+                def _():
+                    y_copy(owner, p, y).start()
 
     def same(a, b):
         return 1 - jnp.minimum((a - b) * (a - b), 1)
@@ -241,7 +253,7 @@
 
     at, value = base_piece(sibling, 0)
     sib_send[1, at] = value.astype(jnp.bfloat16)
-    for p in range(1 + row_steps, PIECES):
+    for p in range(1 + row_steps, PIECES + 1):
         forward(1, p)
     for i in range(1, row_steps):
         at, value = base_piece(sibling, i)
@@ -347,7 +359,9 @@
 
     def y_wait(owner):
         for p in range(PIECES):
-            y_copy(owner, p, other_y).wait_recv()
+            @pl.when(by_y(owner, p))
+            def _():
+                y_copy(owner, p, other_y).wait_recv()
 
     forward(2, 0)
     shrink(order[0])
@@ -356,7 +370,7 @@
         at, value = base_piece(t, i)
         total[at] = value
         forward(2, 2 + i)
-    for p in range(2 + row_steps, PIECES):
+    for p in range(2 + row_steps, PIECES + 1):
         forward(2, p)
     chip_sum(order[0])
     y_wait(order[1])
@@ -371,7 +385,7 @@
     shrink(order[2])
     forward(3, 2)
     expand(order[1])
-    for p in range(3, PIECES):
+    for p in range(3, PIECES + 1):
         forward(3, p)
     chip_sum(order[2])
     for i, half in enumerate(halves):
@@ -390,18 +404,22 @@
         rank_copy(rank_send, rank_sib, owner, 0, sibling).wait_send()
         rank_copy(rank_x_send, rank_x, owner, 1, far).wait_send()
     for owner in range(owners):
-        for p in range(PIECES):
-            @pl.when(owner != z)
-            def _():
-                y_copy(owner, p, y).wait_send()
-
-            @pl.when(jnp.logical_and(owner <= z, z < last))
-            def _():
-                z_copy(owner, p, z + 1, right_sem).wait_send()
-
-            @pl.when(jnp.logical_and(owner >= z, z > 0))
-            def _():
-                z_copy(owner, p, z - 1, left_sem).wait_send()
+        outer = owner in (0, last)
+        for p in range(PIECES + 1 if outer else PIECES):
+            if p < PIECES - 1 or not outer:
+                @pl.when(owner != z)
+                def _():
+                    y_copy(owner, p, y).wait_send()
+
+            if p < PIECES or owner == 0:
+                @pl.when(jnp.logical_and(owner <= z, z < last))
+                def _():
+                    z_copy(owner, p, z + 1, right_sem).wait_send()
+
+            if p < PIECES or owner == last:
+                @pl.when(jnp.logical_and(owner >= z, z > 0))
+                def _():
+                    z_copy(owner, p, z - 1, left_sem).wait_send()
 
 
 def fused(owners, tokens, value_base_matrix, down_table, up_table, adapter_per_block, adapter_position):
@@ -443,17 +461,17 @@
             pltpu.SMEM(adapter_per_block.shape, jnp.int32),
             pltpu.SMEM(adapter_position.shape, jnp.int32),
             dma((8,)),
-            dma((owners, PIECES)),
-            dma((owners, PIECES)),
-            dma((owners, PIECES)),
-            dma((owners, PIECES)),
-            dma((owners, PIECES)),
+            dma((owners, PIECES + 1)),
+            dma((owners, PIECES + 1)),
+            dma((owners, PIECES + 1)),
+            dma((owners, PIECES + 1)),
+            dma((owners, PIECES + 1)),
             dma((2 * (2 * rows // ROWS + 1),)),
             dma((4, owners)),
             dma((6,)),
         ],
         compiler_params=pltpu.CompilerParams(
-            collective_id=0, has_side_effects=True, vmem_limit_bytes=64 * 1024 * 1024
+            collective_id=0, has_side_effects=True, vmem_limit_bytes=60 * 1024 * 1024
         ),
         cost_estimate=pl.CostEstimate(
             flops=2 * rows * feats * (out_columns + width),

time: 38.6 us -> 37.2 us (0.964)
  Pallas kernels: 36.6 us -> 35.1 us
    pallas_call x1, Pallas kernels: 36.6 us -> 35.1 us  [fused(): pl.pallas_call(functools.partial(kernel, owners), out_shape=jax.ShapeDtyp...]
where the time goes in v3:
time: 37.2 us; the launch traced here: 37 us
  Pallas kernels  35.1 us (94%)
  local copies, waits for them, and re-layouts  1.87 us (5%)
    pallas_call x1, Pallas kernels, fused(): pl.pallas_call(functools.partial(kernel, owners), out_shape=jax.ShapeDtyp...  35.1 us
    unnamed x1, local copies, waits for them, and re-layouts  1.87 us

profile of v3, /device:TPU:0, one launch (start us, length us, event | category | flops | bytes accessed | tf_op | source)
XLA Modules:
  0.0 37.0 jit_solution(6207942069488272984)
XLA Ops:
  0.0 35.1 %shard_map.64 = bf16[16,64,256]{2,1,0:T(8,128)(2,1)} custom-call(s32[16]{0:T(128)} %apb_h.1, s32[8]{0:T(128)} %apos_h.1, bf16[16,64,2048]{2,1,0:T(8,128)(2,1)} %bitcast.7, bf16[2048,1024]{1,0:T(8,128)(2,1)} %base_h.1, bf16[128,2048]{1,0:T(8,128)(2,1)} %bitcast.8, bf16[128,256]{1,0:T(8,128)(2,1)} %bitcast.9), custom_call_target="tpu_custom_call" | custom-call | flops 4831838208 | bytes 8912896 | tf_op jit(solution)/shard_map/pallas_call | solution.py:439
  35.1 1.9 %copy.8 = bf16[1024,256]{1,0:T(8,128)(2,1)} copy(bf16[1024,256]{1,0:T(8,128)(2,1)} %bitcast.6) | data formatting | bytes 1048576

commit v4 on v3

--- a/solution.py
+++ b/solution.py
@@ -297,14 +297,17 @@
             for i, to in enumerate((far_sibling, far, sibling))
         ]
 
+    def half_dot(owner, h):
+        features = pl.ds(pl.multiple_of(h * half_feats, half_feats), half_feats)
+        rows = toks[pl.ds(owner * per_owner, per_owner), :, features].reshape(owner_rows, half_feats)
+        return lax.dot_general(
+            rows, table[owner, h, :, width:], (((1,), (1,)), ((), ())), preferred_element_type=jnp.float32
+        )
+
     def shrink(owner, in_one_step=False):
-        rows = toks[pl.ds(owner * per_owner, per_owner)].reshape(owner_rows, feats)
-        value = jnp.zeros((owner_rows, width), jnp.float32)
-        for h in range(2):
-            value = value + lax.dot_general(
-                rows[:, h * half_feats:(h + 1) * half_feats], table[owner, h, :, width:],
-                (((1,), (1,)), ((), ())), preferred_element_type=jnp.float32,
-            )
+        value = half_dot(owner, y)
+        y_wait(owner)
+        value = value + half_dot(owner, other_y)
         picked = []
         for k in range(per_owner):
             rank = value[k * BLK:(k + 1) * BLK, :] * own_lanes(owner, k)
@@ -359,7 +362,7 @@
 
     def y_wait(owner):
         for p in range(PIECES):
-            @pl.when(by_y(owner, p))
+            @pl.when(jnp.logical_and(owner != z, by_y(owner, p)))
             def _():
                 y_copy(owner, p, other_y).wait_recv()
 
@@ -373,7 +376,6 @@
     for p in range(2 + row_steps, PIECES + 1):
         forward(2, p)
     chip_sum(order[0])
-    y_wait(order[1])
     shrink(order[1])
     sib_copy.wait_recv()
     total[...] = total[...] + sib_recv[1].astype(jnp.float32)
@@ -381,7 +383,6 @@
     expand(order[0])
     chip_sum(order[1])
     forward(3, 1)
-    y_wait(order[2])
     shrink(order[2])
     forward(3, 2)
     expand(order[1])
@@ -391,7 +392,6 @@
     for i, half in enumerate(halves):
         x_copy[i].wait_recv()
         total[half] = total[half] + x_recv[half].astype(jnp.float32)
-    y_wait(order[3])
     shrink(order[3], in_one_step=True)
     expand(order[2])
     expand(order[3], in_one_step=True)

time: 37.2 us -> 37.2 us (level)
  no operation moved by 1% of the time
where the time goes in v4:
time: 37.2 us; the launch traced here: 37 us
  Pallas kernels  35.1 us (94%)
  local copies, waits for them, and re-layouts  1.87 us (5%)
    pallas_call x1, Pallas kernels, fused(): pl.pallas_call(functools.partial(kernel, owners), out_shape=jax.ShapeDtyp...  35.1 us
    unnamed x1, local copies, waits for them, and re-layouts  1.87 us

profile of v4, /device:TPU:0, one launch (start us, length us, event | category | flops | bytes accessed | tf_op | source)
XLA Modules:
  0.0 37.0 jit_solution(2890739969050435019)
XLA Ops:
  0.0 35.1 %shard_map.64 = bf16[16,64,256]{2,1,0:T(8,128)(2,1)} custom-call(s32[16]{0:T(128)} %apb_h.1, s32[8]{0:T(128)} %apos_h.1, bf16[16,64,2048]{2,1,0:T(8,128)(2,1)} %bitcast.7, bf16[2048,1024]{1,0:T(8,128)(2,1)} %base_h.1, bf16[128,2048]{1,0:T(8,128)(2,1)} %bitcast.8, bf16[128,256]{1,0:T(8,128)(2,1)} %bitcast.9), custom_call_target="tpu_custom_call" | custom-call | flops 4831838208 | bytes 8912896 | tf_op jit(solution)/shard_map/pallas_call | solution.py:439
  35.1 1.9 %copy.8 = bf16[1024,256]{1,0:T(8,128)(2,1)} copy(bf16[1024,256]{1,0:T(8,128)(2,1)} %bitcast.6) | data formatting | bytes 1048576
